TPU v7x, 32 devices: a whole 2x2x4 slice. The times are simulated.
32 devices in a mesh: tm: 16 (over z, y, core), chan: 2 (over x).
Axes of the slice: x: 2, y: 2, z: 4, core: 2. Of those that a mesh axis runs over, the one named last changes fastest.
Arguments:
- clip_input: bfloat16 [512, 32, 256], P('chan', 'tm'), may hold values from -16 to 16, as said below
- lengths: int32 [8], replicated, may hold values from 1 to 16, 32 in all
- gamma_one: float32 [512], P('chan'), may hold values from 0.25 to 1.75
- beta_one: float32 [512], P('chan'), may hold values from -1.5 to 1.5
- w_one: bfloat16 [512, 27, 512], P('chan'), may hold values from -0.0546875 to 0.0546875
- bias_one: float32 [512], P('chan'), may hold values from -1.5 to 1.5
- gamma_two: float32 [512], P('chan'), may hold values from 0.25 to 1.75
- beta_two: float32 [512], P('chan'), may hold values from -1.5 to 1.5
- w_two: bfloat16 [512, 27, 512], P('chan'), may hold values from -0.0546875 to 0.0546875
- bias_two: float32 [512], P('chan'), may hold values from -1.5 to 1.5
Outputs:
- block_output: float32 [512, 32, 256], P('chan', 'tm')
Inputs may be any that keep to these rules, and one draw needn't show every extreme that they name: `clip_input`: activations of order one. `lengths`: the 8 counts sum to 32; the longest is exactly 16.
All inputs are finite; a program needn't handle non-finite values.
Results may differ from a plain program's by a relative error of at most 0.0054.
Values may be sent and summed in bfloat16 or wider, within the bound.
A program may use at most 128 MiB of HBM per device.

v0:
```python
import jax
import jax.numpy as jnp
from jax import lax
from jax.sharding import PartitionSpec as P

C = 512
GROUPS = 32
H = 16
W = 16


EPS = 1e-06


def shifted(value, axis, steps):
    count = lax.axis_size(axis)
    first, last = (max(0, -steps), min(count, count - steps))
    return lax.ppermute(value, axis, [(source, source + steps) for source in range(first, last)])


def clip_member(frames, ends, nclips):
    clips = jnp.sum((frames[:, None] >= ends[None, :]).astype(jnp.int32), axis=1)
    member = (clips[:, None] == jnp.arange(nclips, dtype=jnp.int32)[None, :]).astype(jnp.int32)
    return member


def local_sums(data, member):
    chans, frames, cells = data.shape
    group_size = C // GROUPS
    grouped = data.reshape(chans // group_size, group_size, frames, cells)
    sums = jnp.sum(grouped, axis=(1, 3))
    squares = jnp.sum(grouped * grouped, axis=(1, 3))
    weights = member.astype(jnp.float32)
    return (
        jnp.dot(sums, weights, precision=lax.Precision.HIGHEST),
        jnp.dot(squares, weights, precision=lax.Precision.HIGHEST),
    )


def apply_norm(data, mean, scale, member, gamma, beta):
    chans, frames, cells = data.shape
    group_size = C // GROUPS
    weights = member.astype(jnp.float32)
    mean_f = jnp.dot(mean, weights.T, precision=lax.Precision.HIGHEST)
    scale_f = jnp.dot(scale, weights.T, precision=lax.Precision.HIGHEST)
    grouped = data.reshape(chans // group_size, group_size, frames, cells)
    normed = (grouped - mean_f[:, None, :, None]) * scale_f[:, None, :, None]
    normed = normed.reshape(chans, frames, cells) * gamma[:, None, None] + beta[:, None, None]
    return jax.nn.silu(normed).astype(jnp.bfloat16)


def conv_taps(weight_rows, extended, keep):
    rows, span, cells = extended.shape
    count = span - 2
    padded = jnp.pad(extended.reshape(rows, span, H, W), ((0, 0), (0, 0), (1, 1), (1, 1)))
    total = None
    for kt in range(3):
        for kh in range(3):
            for kw in range(3):
                piece = (
                    padded[:, kt : kt + count, kh : kh + H, kw : kw + W]
                    * keep[kt][None, :, None, None]
                )
                term = lax.dot_general(
                    weight_rows[:, 9 * kt + 3 * kh + kw, :],
                    piece.reshape(rows, count * H * W),
                    (((0,), (0,)), ((), ())),
                    preferred_element_type=jnp.float32,
                )
                total = term if total is None else total + term
    return total


def block_layer(raw, gamma, beta, weight, bias, own_member, counts, keep):
    chans, frames, cells = raw.shape
    data = raw.astype(jnp.float32)
    sums, squares = lax.psum(local_sums(data, own_member), "tm")
    mean = sums / counts[None, :]
    var = squares / counts[None, :] - mean * mean
    scale = lax.rsqrt(var + EPS)
    hidden = apply_norm(data, mean, scale, own_member, gamma, beta)
    tail = shifted(hidden, "tm", 1)
    extended = jnp.concatenate([tail, hidden], axis=1)
    summed = lax.psum(conv_taps(weight, extended, keep), "chan")
    own = lax.dynamic_slice_in_dim(summed, lax.axis_index("chan") * chans, chans, 0)
    return own.reshape(chans, frames, cells) + bias[:, None, None]


def on_device(
    clip_input, lengths, gamma_one, beta_one, w_one, bias_one, gamma_two, beta_two, w_two, bias_two
):
    chans, frames, cells = clip_input.shape
    nclips = lengths.shape[0]
    ends = jnp.cumsum(lengths)
    starts = ends - lengths
    first_frame = lax.axis_index("tm") * frames
    own_frames = first_frame + jnp.arange(frames, dtype=jnp.int32)
    own_member = clip_member(own_frames, ends, nclips)
    clip_start = jnp.sum(own_member * starts[None, :], axis=1)
    keep = jnp.stack([own_frames - 2 + kt >= clip_start for kt in range(3)], axis=0).astype(
        jnp.bfloat16
    )
    counts = lengths.astype(jnp.float32) * float(C // GROUPS * H * W)
    y_one = block_layer(clip_input, gamma_one, beta_one, w_one, bias_one, own_member, counts, keep)
    y_one = y_one.astype(jnp.bfloat16)
    y_two = block_layer(y_one, gamma_two, beta_two, w_two, bias_two, own_member, counts, keep)
    return clip_input.astype(jnp.float32) + y_two


def solution(mesh):
    in_specs = (
        P("chan", "tm", None),
        P(),
        P("chan"),
        P("chan"),
        P("chan", None, None),
        P("chan"),
        P("chan"),
        P("chan"),
        P("chan", None, None),
        P("chan"),
    )
    out_specs = P("chan", "tm", None)
    return jax.shard_map(
        on_device, mesh=mesh, in_specs=in_specs, out_specs=out_specs, check_vma=False
    )
```

profile of v0, /device:TPU:0, one launch (start us, length us, event | category | flops | bytes accessed | tf_op | source)
XLA Modules:
  0.0 202.2 jit_solution(6125349171889313229)
XLA Ops:
  6.5 1.1 copy.24
  8.1 0.7 convert_multiply_fusion.2
  8.7 0.8 reduce-window.8
  10.3 35.4 %all-reduce.3 = (f32[16,8]{0,1:T(8,128)S(1)}, f32[16,8]{0,1:T(8,128)S(1)}) all-reduce(f32[16,8]{0,1:T(8,128)S(1)} %fusion.216, f32[16,8]{0,1:T(8,128)S(1)} %fusion.220), channel_id=1, replica_groups=mesh['tm'=16,'chan'=2] {'tm'}, use_global_device_ids=true, to_apply=%region_7.8 | all-reduce | flops 256 | bytes 2048 | tf_op jit(solution)/shard_map/psum | solution.py:77
  46.5 1.0 fusion.31
  47.5 1.6 collective-permute-start
  49.1 0.7 bitcast_subtract_fusion
  50.3 0.4 fusion.40
  50.7 0.4 fusion.48
  51.2 0.3 fusion.55
  51.8 0.3 convolution_bitcast_fusion.18
  52.4 0.3 convolution_bitcast_fusion.14
  58.5 0.3 fusion.3
  59.4 1.3 fusion.9
  60.9 39.0 %all-reduce.7.cloned.1.call-done = f32[512,512]{0,1:T(8,128)} async-done(((f32[512,512]{0,1:T(8,128)}), f32[512,512]{0,1:T(8,128)}) %all-reduce.7.cloned.1.call-update) | async-done | bytes 1048592 | tf_op jit(solution)/shard_map/psum | solution.py:84
  100.0 1.1 constant_dynamic-slice_fusion
  101.0 1.0 copy.25
  102.0 2.2 %reshape.305 = f32[16,16,2,256]{3,2,1,0:T(2,128)} reshape(f32[256,512]{1,0:T(8,128)} %copy.25) | data formatting | bytes 1048576 | tf_op jit(solution)/shard_map/reshape | solution.py:86
  104.2 1.7 convert_reduce_fusion.1
  106.4 33.7 %all-reduce.2 = (f32[16,8]{0,1:T(8,128)S(1)}, f32[16,8]{0,1:T(8,128)S(1)}) all-reduce(f32[16,8]{0,1:T(8,128)S(1)} %fusion.209, f32[16,8]{0,1:T(8,128)S(1)} %fusion.213), channel_id=1, replica_groups=mesh['tm'=16,'chan'=2] {'tm'}, use_global_device_ids=true, to_apply=%region_13.14 | all-reduce | flops 256 | bytes 2048 | tf_op jit(solution)/shard_map/psum | solution.py:77
  141.1 1.5 collective-permute-start.1
  142.6 0.9 collective-permute-done.1
  143.6 0.4 fusion.64
  144.0 0.4 fusion.72
  144.5 0.3 fusion.79
  144.8 0.9 slice-done.1
  147.6 0.3 convolution_add_fusion.15
  153.2 0.3 fusion.17
  153.5 1.3 fusion.19
  154.9 38.3 %all-reduce.9.cloned.1.call-done = f32[512,512]{0,1:T(8,128)} async-done(((f32[512,512]{0,1:T(8,128)}), f32[512,512]{0,1:T(8,128)}) %all-reduce.9.cloned.1.call-update) | async-done | bytes 1048592 | tf_op jit(solution)/shard_map/psum | solution.py:84
  193.2 1.1 constant_dynamic-slice_fusion.1
  194.4 1.0 copy.26
  (102 shorter events, 17.9 us)
Async XLA Ops:
  6.5 93.4 %all-reduce.7.cloned.1.call-start = ((), (), s32[]{:S(2)}) async-start(), calls=%async_computation | async-start | bytes 2097152 | tf_op jit(solution)/shard_map/psum | solution.py:84
  7.6 44.5 %copy-start.1 = (bf16[256,2,256]{0,2,1:T(8,128)(2,1)}, bf16[256,2,256]{0,2,1:T(8,128)(2,1)S(1)}, u32[]{:S(2)}) copy-start(bf16[256,2,256]{0,2,1:T(8,128)(2,1)S(1)} %copy.24) | copy-start | bytes 786436
  46.5 5.0 %copy-start = (bf16[256,27,512]{2,0,1:T(8,128)(2,1)S(1)}, bf16[256,27,512]{2,0,1:T(8,128)(2,1)}, u32[]{:S(2)}) copy-start(bf16[256,27,512]{2,0,1:T(8,128)(2,1)} %param.14) | copy-start | bytes 21233668
  47.5 2.7 %collective-permute-start = (bf16[256,2,256]{0,2,1:T(8,128)(2,1)S(1)}, bf16[256,2,256]{0,2,1:T(8,128)(2,1)S(1)}, u32[]{:S(2)}, u32[]{:S(2)}) collective-permute-start(bf16[256,2,256]{0,2,1:T(8,128)(2,1)S(1)} %fusion.31), channel_id=1, source_target_pairs={{0,2},{2,4},{4,6},{6,8},{8,10},{10,12},{12,14},{14,16},{16,18},{18... | collective-permute-start | bytes 786440 | tf_op jit(solution)/shard_map/ppermute | solution.py:18
  58.5 2.4 %copy-start.3 = (f32[256]{0:T(256)S(1)}, f32[256]{0:T(256)}, u32[]{:S(2)}) copy-start(f32[256]{0:T(256)} %param.15) | copy-start | bytes 3076
  59.1 81.8 %copy-start.4 = (f32[256]{0:T(256)S(1)}, f32[256]{0:T(256)}, u32[]{:S(2)}) copy-start(f32[256]{0:T(256)} %param.17) | copy-start | bytes 3076
  59.1 81.8 %copy-start.5 = (f32[256]{0:T(256)S(1)}, f32[256]{0:T(256)}, u32[]{:S(2)}) copy-start(f32[256]{0:T(256)} %param.16) | copy-start | bytes 3076
  60.8 132.4 %all-reduce.9.cloned.1.call-start = ((), (), s32[]{:S(2)}) async-start(), calls=%async_computation.1 | async-start | bytes 2097152 | tf_op jit(solution)/shard_map/psum | solution.py:84
  101.0 43.8 %slice-start = ((s8[7077888]{0:T(1024)(128)(4,1)}), s8[2883584]{0:T(1024)(128)(4,1)S(1)}, s32[]{:S(2)}) async-start(s8[7077888]{0:T(1024)(128)(4,1)} %bitcast.393), calls=%async_computation.2 | async-start | bytes 5767168
  141.1 2.4 %collective-permute-start.1 = (bf16[256,2,256]{0,2,1:T(8,128)(2,1)S(1)}, bf16[256,2,256]{0,2,1:T(8,128)(2,1)S(1)}, u32[]{:S(2)}, u32[]{:S(2)}) collective-permute-start(bf16[256,2,256]{0,2,1:T(8,128)(2,1)S(1)} %multiply_convert_fusion), channel_id=1, source_target_pairs={{0,2},{2,4},{4,6},{6,8},{8,10},{10,12},{12,14},{14,16},{16,18},{18... | collective-permute-start | bytes 786440 | tf_op jit(solution)/shard_map/ppermute | solution.py:18
  143.6 2.2 %slice-start.1 = ((s8[7077888]{0:T(1024)(128)(4,1)}), s8[4194304]{0:T(1024)(128)(4,1)S(1)}, s32[]{:S(2)}) async-start(s8[7077888]{0:T(1024)(128)(4,1)} %bitcast.393), calls=%async_computation.3 | async-start | bytes 8388608
  152.9 41.4 %copy-start.2 = (bf16[256,2,256]{0,2,1:T(8,128)(2,1)S(1)}, bf16[256,2,256]{0,2,1:T(8,128)(2,1)}, u32[]{:S(2)}) copy-start(bf16[256,2,256]{0,2,1:T(8,128)(2,1)} %copy-done.1) | copy-start | bytes 786436
  152.9 41.4 %copy-start.6 = (f32[256]{0:T(256)S(1)}, f32[256]{0:T(256)}, u32[]{:S(2)}) copy-start(f32[256]{0:T(256)} %param.19) | copy-start | bytes 3076
Sparse Core Ops, SparseCore 0:
  60.9 39.0 all-reduce.6
  155.0 38.1 all-reduce.8
where the time goes:
time: 203 us; the launch traced here: 202 us
  waiting for transfers between devices  78.6 us (39%)
  blocking collectives  69.1 us (34%)
  matrix products  19.8 us (10%)
  between operations  14 us (7%)
  local copies, waits for them, and re-layouts  9.32 us (5%)
  other arithmetic  8.31 us (4%)
  starting transfers between devices  3.1 us (2%)
    psum x2, waiting for transfers between devices, block_layer(): summed = lax.psum(conv_taps(weight, extended, keep), 'chan')  77.3 us
    psum x2, blocking collectives, block_layer(): sums, squares = lax.psum(local_sums(data, own_member), 'tm')  69.1 us
    dot_general x54, matrix products, conv_taps(): lax.dot_general(weight_rows[:, 9 * kt + 3 * kh + kw, :], piece.reshape(ro...  18 us
  transfers between devices with their start and end apart: 4, of which 4 were waited for; matrix products, arithmetic and copies ran while one was open for 0% of the time, Pallas kernels for 0%

commit v1 on v0

v1 whole, which is shorter than its diff:
```python
import functools

import jax
import jax.numpy as jnp
from jax import lax
from jax.experimental import pallas as pl
from jax.experimental.pallas import tpu as pltpu
from jax.sharding import PartitionSpec as P

C = 512
GROUPS = 32
SIZE = C // GROUPS
H = 16
W = 16
CELLS = H * W
PAD = CELLS + 2 * W
EPS = 1e-06
MESH = pl.DeviceIdType.MESH
HIGHEST = lax.Precision.HIGHEST


def iota(shape, dim):
    return lax.broadcasted_iota(jnp.int32, shape, dim)


def dot(a, b, precision=None):
    return lax.dot_general(
        a, b, (((1,), (0,)), ((), ())), precision=precision, preferred_element_type=jnp.float32
    )


def kernel(
    n, T, nclip, wide,
    len_ref, x_ref, par_ref, w1_ref, w2_ref, out_ref,
    wbuf, hs, halo, stats, psend, precv, y_ref,
    w_sem, hsend, hrecv, ssend, srecv, qsend, qrecv,
):
    ci = x_ref.shape[1]
    me = lax.axis_index("tm")
    ch = lax.axis_index("chan")
    rows = 2 * CELLS

    def peer(d):
        return lax.rem(me + d, T), ch

    def partner(k):
        return me, lax.rem(ch + k, n)

    def w_copy(layer, k, part):
        w_ref = (w1_ref, w2_ref)[layer]
        tgt = lax.rem(ch + k, n)
        taps = pl.ds(9 * part, 9)
        if wide:
            src = w_ref.at[taps, :, pl.ds(pl.multiple_of(tgt * ci, ci), ci)]
        else:
            src = w_ref.at[tgt, taps]
        return pltpu.make_async_copy(src, wbuf.at[layer, k, taps], w_sem.at[layer, k, part])

    order = list(range(1, n)) + [0]
    for layer in range(2):
        for k in order:
            for part in (2, 1, 0):
                w_copy(layer, k, part).start()

    barrier = pltpu.get_barrier_semaphore()

    def greet(d, carry):
        pl.semaphore_signal(barrier, inc=1, device_id=peer(d), device_id_type=MESH)
        return carry

    lax.fori_loop(1, T, greet, 0)
    for k in range(1, n):
        pl.semaphore_signal(barrier, inc=1, device_id=partner(k), device_id_type=MESH)

    hs[:, :, :, 0:W, :] = jnp.zeros((3, 3, 2, W, ci), jnp.bfloat16)
    hs[:, :, :, W + CELLS :, :] = jnp.zeros((3, 3, 2, W, ci), jnp.bfloat16)

    @pl.when(me == 0)
    def _():
        halo[...] = jnp.zeros_like(halo)

    first = 2 * me
    starts, counts, spans = [], [], []
    for f in range(4):
        g = first - 2 + f
        begin = jnp.int32(0)
        count = jnp.int32(0)
        run = jnp.int32(0)
        for c in range(nclip):
            size = len_ref[c]
            inside = jnp.logical_and(run <= g, g < run + size)
            begin = jnp.where(inside, run, begin)
            count = jnp.where(inside, size, count)
            run = run + size
        starts.append(begin)
        counts.append(count)
        spans.append((begin, begin + count))

    def halo_copy(layer):
        src = x_ref if layer == 0 else y_ref
        return pltpu.make_async_remote_copy(
            src_ref=src, dst_ref=halo.at[layer],
            send_sem=hsend.at[layer], recv_sem=hrecv.at[layer],
            device_id=peer(1), device_id_type=MESH,
        )

    def stat_copy(layer, d):
        return pltpu.make_async_remote_copy(
            src_ref=stats.at[layer, me], dst_ref=stats.at[layer, me],
            send_sem=ssend.at[layer, d], recv_sem=srecv.at[layer, d],
            device_id=peer(d), device_id_type=MESH,
        )

    def part_copy(layer, k):
        return pltpu.make_async_remote_copy(
            src_ref=psend.at[layer, k - 1], dst_ref=precv.at[layer, k - 1],
            send_sem=qsend.at[layer, k - 1], recv_sem=qrecv.at[layer, k - 1],
            device_id=partner(k), device_id_type=MESH,
        )

    lane_group = (iota((ci, 128), 1) % 32 == iota((ci, 128), 0) // SIZE).astype(jnp.float32)
    lane_t = iota((128, ci), 0)
    member = lane_t % 32 == iota((128, ci), 1) // SIZE
    pick_sum = jnp.logical_and(member, lane_t < 64).astype(jnp.float32)
    pick_sq = jnp.logical_and(member, lane_t >= 64).astype(jnp.float32)

    def local_stats(layer, a, b):
        lines = [
            jnp.sum(v, axis=0, keepdims=True) for v in (a, b, a * a, b * b)
        ] + [jnp.zeros((4, ci), jnp.float32)]
        by_group = dot(jnp.concatenate(lines, axis=0), lane_group, HIGHEST)
        own = iota((8, 128), 0) == iota((8, 128), 1) // 32
        stats[layer, me] = jnp.sum(jnp.where(own, by_group, 0.0), axis=0, keepdims=True)

    def send_stats(layer):
        def go(d, carry):
            stat_copy(layer, d).start()
            return carry

        lax.fori_loop(1, T, go, 0)

    def clip_stats(layer):
        def come(d, carry):
            stat_copy(layer, d).wait_recv()
            return carry

        lax.fori_loop(1, T, come, 0)
        every = stats[layer]
        frame = 2 * iota((T, 1, 128), 0) + (iota((T, 1, 128), 2) // 32) % 2
        lines = []
        for f in range(4):
            low, high = spans[f]
            inside = jnp.logical_and(frame >= low, frame < high)
            total = jnp.sum(jnp.where(inside, every, 0.0), axis=0)
            cells = jnp.maximum(counts[f], 1).astype(jnp.float32) * float(SIZE * CELLS)
            lines.append(total / jnp.full((1, 128), cells))
        lines = jnp.concatenate(lines + [jnp.zeros((4, 128), jnp.float32)], axis=0)
        mean = dot(lines, pick_sum, HIGHEST)
        var = dot(lines, pick_sq, HIGHEST) - mean * mean
        return mean, lax.rsqrt(var + EPS)

    column = iota((CELLS, ci), 0) % W

    def place(layer, f, data, mean, scale, slots):
        gamma = par_ref[3 * layer : 3 * layer + 1, :]
        beta = par_ref[3 * layer + 1 : 3 * layer + 2, :]
        u = (data - mean[f : f + 1]) * (scale[f : f + 1] * gamma) + beta
        h = 0.5 * u * (1.0 + jnp.tanh(0.5 * u))
        before = jnp.where(column == 0, 0.0, pltpu.roll(h, 1, 0))
        after = jnp.where(column == W - 1, 0.0, pltpu.roll(h, CELLS - 1, 0))
        for kw, v in enumerate((before, h, after)):
            for kt, j in slots:
                if kt == 2:
                    kept = v
                else:
                    keep = jnp.full((CELLS, ci), starts[2 + j]) <= first + (j - 2 + kt)
                    kept = jnp.where(keep, v, 0.0)
                hs[kw, kt, j, W : W + CELLS, :] = kept.astype(jnp.bfloat16)

    def taps(layer, k, kt):
        w_copy(layer, k, kt).wait()
        if ci % 128 == 0:
            pieces = [
                hs[kw, kt, :, kh * W : kh * W + CELLS, :].reshape(rows, ci)
                for kh in range(3)
                for kw in range(3)
            ]
            weights = wbuf[layer, k, 9 * kt : 9 * kt + 9].reshape(9 * ci, ci)
            return dot(jnp.concatenate(pieces, axis=1), weights)
        total = None
        for kh in range(3):
            for kw in range(3):
                piece = hs[kw, kt, :, kh * W : kh * W + CELLS, :].reshape(rows, ci)
                term = dot(piece, wbuf[layer, k, 9 * kt + 3 * kh + kw])
                total = term if total is None else total + term
        return total

    def convolve(layer, a, b):
        local_stats(layer, a, b)
        send_stats(layer)
        mean, scale = clip_stats(layer)
        place(layer, 2, a, mean, scale, [(2, 0), (1, 1)])
        place(layer, 3, b, mean, scale, [(2, 1)])
        own = None
        for k in order:
            total = taps(layer, k, 2)
            if k == order[0]:

                @pl.when(me > 0)
                def _():
                    halo_copy(layer).wait_recv()

                place(layer, 0, halo[layer, 0:CELLS, :].astype(jnp.float32), mean, scale, [(0, 0)])
                place(
                    layer, 1, halo[layer, CELLS:, :].astype(jnp.float32), mean, scale,
                    [(1, 0), (0, 1)],
                )
            total = total + taps(layer, k, 1) + taps(layer, k, 0)
            if k:
                psend[layer, k - 1] = total.astype(jnp.bfloat16)
                part_copy(layer, k).start()
            else:
                own = total
        own = own + par_ref[3 * layer + 2 : 3 * layer + 3, :]
        for k in range(1, n):
            part_copy(layer, k).wait_recv()
            own = own + precv[layer, k - 1].astype(jnp.float32)
        return own

    pl.semaphore_wait(barrier, T - 1 + n - 1)

    @pl.when(me < T - 1)
    def _():
        halo_copy(0).start()

    x = x_ref[...].astype(jnp.float32)
    y_ref[...] = convolve(0, x[:CELLS], x[CELLS:]).astype(jnp.bfloat16)

    @pl.when(me < T - 1)
    def _():
        halo_copy(1).start()

    y = y_ref[...].astype(jnp.float32)
    z = convolve(1, y[:CELLS], y[CELLS:])
    out_ref[...] = x_ref[...].astype(jnp.float32) + z

    for layer in range(2):

        @pl.when(me < T - 1)
        def _():
            halo_copy(layer).wait_send()

        def sent(d, carry):
            stat_copy(layer, d).wait_send()
            return carry

        lax.fori_loop(1, T, sent, 0)
        for k in range(1, n):
            part_copy(layer, k).wait_send()


def on_device(n, T, x, lengths, g1, b1, w1, c1, g2, b2, w2, c2):
    ci, frames, cells = x.shape
    rows = frames * cells
    wide = ci % 128 == 0
    if wide:
        w1, w2 = [w.transpose(1, 0, 2) for w in (w1, w2)]
    else:
        w1, w2 = [w.reshape(ci, 27, n, ci).transpose(2, 1, 0, 3) for w in (w1, w2)]
    zero = jnp.zeros_like(g1)
    par = jnp.stack([g1, b1, c1, g2, b2, c2, zero, zero])
    xt = x.transpose(1, 2, 0).reshape(rows, ci)
    vmem = pl.BlockSpec(memory_space=pltpu.VMEM)
    hbm = pl.BlockSpec(memory_space=pl.ANY)
    dma = pltpu.SemaphoreType.DMA
    out = pl.pallas_call(
        functools.partial(kernel, n, T, lengths.shape[0], wide),
        out_shape=jax.ShapeDtypeStruct((rows, ci), jnp.float32),
        in_specs=[pl.BlockSpec(memory_space=pltpu.SMEM), vmem, vmem, hbm, hbm],
        out_specs=vmem,
        scratch_shapes=[
            pltpu.VMEM((2, n, 27, ci, ci), jnp.bfloat16),
            pltpu.VMEM((3, 3, 2, PAD, ci), jnp.bfloat16),
            pltpu.VMEM((2, rows, ci), jnp.bfloat16),
            pltpu.VMEM((2, T, 1, 128), jnp.float32),
            pltpu.VMEM((2, n - 1, rows, ci), jnp.bfloat16),
            pltpu.VMEM((2, n - 1, rows, ci), jnp.bfloat16),
            pltpu.VMEM((rows, ci), jnp.bfloat16),
            dma((2, n, 3)),
            dma((2,)),
            dma((2,)),
            dma((2, T)),
            dma((2, T)),
            dma((2, n - 1)),
            dma((2, n - 1)),
        ],
        compiler_params=pltpu.CompilerParams(
            collective_id=0, has_side_effects=True, vmem_limit_bytes=56 * 2**20
        ),
        cost_estimate=pl.CostEstimate(
            flops=4 * 27 * ci * C * rows, bytes_accessed=4 * 27 * ci * C, transcendentals=0
        ),
    )(lengths, xt, par, w1, w2)
    return out.reshape(frames, cells, ci).transpose(2, 0, 1)


def solution(mesh):
    n, T = mesh.shape["chan"], mesh.shape["tm"]
    c = P("chan")
    cube = P("chan", None, None)
    data = P("chan", "tm", None)
    return jax.shard_map(
        functools.partial(on_device, n, T),
        mesh=mesh,
        in_specs=(data, P(), c, c, cube, c, c, c, cube, c),
        out_specs=data,
        check_vma=False,
    )
```

time: 203 us -> 48.6 us (0.24)
  waiting for transfers between devices: 78.6 us -> 0 us
  blocking collectives: 69.1 us -> 0 us
  Pallas kernels: 0 us -> 43.2 us
  matrix products: 19.8 us -> 0 us
  between operations: 14 us -> 0.01 us
  other arithmetic: 8.31 us -> 0 us
  local copies, waits for them, and re-layouts: 9.32 us -> 5.22 us
  starting transfers between devices: 3.1 us -> 0 us
    psum x2 -> x0, waiting for transfers between devices: 77.3 us -> none  [block_layer(): summed = lax.psum(conv_taps(weight, extended, keep), 'chan')]
    psum x2 -> x0, blocking collectives: 69.1 us -> none  [block_layer(): sums, squares = lax.psum(local_sums(data, own_member), 'tm')]
    pallas_call x0 -> x1, Pallas kernels: none -> 43.2 us  [on_device(): pl.pallas_call(functools.partial(kernel, n, T, lengths.shape[0], wide), o...]
    dot_general x62 -> x0, matrix products: 19.8 us -> none  [the longest x54 18 us: conv_taps(): lax.dot_general(weight_rows[:, 9 * kt + 3 * kh + kw, :], piece.reshape(ro...]
    dynamic_slice x3 -> x0, local copies, waits for them, and re-layouts: 3.15 us -> none  [block_layer(): lax.dynamic_slice_in_dim(summed, lax.axis_index('chan') * chans, chans, 0)]
    mul x7 -> x0, other arithmetic: 3.1 us -> none  [the longest x6 2.43 us: conv_taps(): padded[:, kt:kt + count, kh:kh + H, kw:kw + W]]
    ppermute x2 -> x0, starting transfers between devices: 3.06 us -> none  [shifted(): lax.ppermute(value, axis, [(source, source + steps) for source in range(f...]
    reduce_sum x6 -> x0, other arithmetic: 2.29 us -> none  [the longest x3 1.84 us: local_sums(): sums = jnp.sum(grouped, axis=(1, 3))]
  transfers between devices with their start and end apart: 4 -> 0, of which waited for: 4 -> 0; matrix products, arithmetic and copies ran while one was open for 0% -> 0% of each run, Pallas kernels for 0% -> 0%
where the time goes in v1:
time: 48.6 us; the launch traced here: 48.4 us
  Pallas kernels  43.2 us (89%)
  local copies, waits for them, and re-layouts  5.22 us (11%)
    pallas_call x1, Pallas kernels, on_device(): pl.pallas_call(functools.partial(kernel, n, T, lengths.shape[0], wide), o...  43.2 us
    reshape x1, local copies, waits for them, and re-layouts, on_device(): return out.reshape(frames, cells, ci).transpose(2, 0, 1)  2.04 us
    transpose x1, local copies, waits for them, and re-layouts, on_device(): xt = x.transpose(1, 2, 0).reshape(rows, ci)  1.81 us
    another operation x2, local copies, waits for them, and re-layouts, on_device(): par = jnp.stack([g1, b1, c1, g2, b2, c2, zero, zero])  1.37 us

profile of v1, /device:TPU:0, one launch (start us, length us, event | category | flops | bytes accessed | tf_op | source)
XLA Modules:
  0.0 48.4 jit_solution(3296015265067334677)
XLA Ops:
  0.0 1.4 %stack.31.par_ref = f32[8,256]{1,0:T(8,128)} concatenate(f32[1,256]{1,0:T(1,128)} %bitcast.15, f32[1,256]{1,0:T(1,128)} %bitcast.16, f32[1,256]{1,0:T(1,128)} %bitcast.17, f32[1,256]{1,0:T(1,128)} %bitcast.18, f32[1,256]{1,0:T(1,128)} %bitcast.19, f32[1,256]{1,0:T(1,128)} %bitcast.20, f32[2,256]{1,0:T(2,128)S(1)} %stack.30), dimensions={0} | concatenate | bytes 16384 | tf_op jit(solution)/shard_map/stack | solution.py:271
  1.4 1.8 %copy.11 = bf16[2,256,256]{2,1,0:T(8,128)(2,1)} copy(bf16[2,256,256]{1,0,2:T(2,128)(2,1)} %bitcast.13) | data formatting | bytes 524288 | tf_op jit(solution)/shard_map/transpose | solution.py:272
  3.2 43.2 %shard_map.100 = f32[512,256]{1,0:T(8,128)} custom-call(s32[8]{0:T(128)} %len_ref.1, bf16[512,256]{1,0:T(8,128)(2,1)} %bitcast.14, f32[8,256]{1,0:T(8,128)} %stack.31.par_ref, bf16[27,256,512]{2,1,0:T(8,128)(2,1)} %bitcast.21, bf16[27,256,512]{2,1,0:T(8,128)(2,1)} %bitcast.22), custom_call_target="tpu_custom_call" | custom-call | flops 7247757312 | bytes 14155776 | tf_op jit(solution)/shard_map/pallas_call | solution.py:276
  46.4 2.0 %copy.12 = f32[2,256,256]{1,0,2:T(2,128)} copy(f32[2,256,256]{2,1,0:T(8,128)} %bitcast.12) | data formatting | bytes 1048576 | tf_op jit(solution)/shard_map/reshape | solution.py:304
  (1 shorter events, 0.0 us)

commit v2 on v1

v2 whole, which is shorter than its diff:
```python
import functools

import jax
import jax.numpy as jnp
from jax import lax
from jax.experimental import pallas as pl
from jax.experimental.pallas import tpu as pltpu
from jax.sharding import PartitionSpec as P

C = 512
GROUPS = 32
SIZE = C // GROUPS
H = 16
W = 16
CELLS = H * W
PAD = CELLS + 2 * W
EPS = 1e-06
MESH = pl.DeviceIdType.MESH


def iota(shape, dim):
    return lax.broadcasted_iota(jnp.int32, shape, dim)


def dot(a, b):
    return lax.dot_general(a, b, (((1,), (0,)), ((), ())), preferred_element_type=jnp.float32)


def kernel(
    n, T, nclip, wide,
    len_ref, x_ref, g1_ref, b1_ref, c1_ref, g2_ref, b2_ref, c2_ref, w1_ref, w2_ref, out_ref,
    wbuf, hs, halo, stats, lines, psend, precv, ybuf, par,
    w_sem, in_sem, hsend, hrecv, ssend, srecv, qsend, qrecv,
):
    ci = x_ref.shape[2]
    me = lax.axis_index("tm")
    ch = lax.axis_index("chan")

    def peer(d):
        return lax.rem(me + d, T), ch

    def partner(k):
        return me, lax.rem(ch + k, n)

    def w_copy(w_ref, layer, k):
        tgt = lax.rem(ch + k, n)
        if wide:
            src = w_ref.at[:, :, pl.ds(pl.multiple_of(tgt * ci, ci), ci)]
        else:
            src = w_ref.at[tgt]
        return pltpu.make_async_copy(src, wbuf.at[layer, k], w_sem.at[layer, k])

    loads = [pltpu.make_async_copy(x_ref, ybuf.at[0], in_sem.at[6])] + [
        pltpu.make_async_copy(ref, par.at[i], in_sem.at[i])
        for i, ref in enumerate((g1_ref, b1_ref, c1_ref, g2_ref, b2_ref, c2_ref))
    ]
    for load in loads:
        load.start()

    barrier = pltpu.get_barrier_semaphore()

    def greet(d, carry):
        pl.semaphore_signal(barrier, inc=1, device_id=peer(d), device_id_type=MESH)
        return carry

    lax.fori_loop(1, T, greet, 0)
    for k in range(1, n):
        pl.semaphore_signal(barrier, inc=1, device_id=partner(k), device_id_type=MESH)

    for layer, w_ref in enumerate((w1_ref, w2_ref)):
        for k in list(range(1, n)) + [0]:
            w_copy(w_ref, layer, k).start()

    hs[:, :, 0:W, :] = jnp.zeros((3, 2, W, 3 * ci), jnp.bfloat16)
    hs[:, :, W + CELLS :, :] = jnp.zeros((3, 2, W, 3 * ci), jnp.bfloat16)

    @pl.when(me == 0)
    def _():
        halo[...] = jnp.zeros_like(halo)

    first = 2 * me
    starts, counts = [], []
    for f in range(4):
        g = first - 2 + f
        begin = jnp.int32(0)
        count = jnp.int32(0)
        run = jnp.int32(0)
        for c in range(nclip):
            size = len_ref[c]
            inside = jnp.logical_and(run <= g, g < run + size)
            begin = jnp.where(inside, run, begin)
            count = jnp.where(inside, size, count)
            run = run + size
        starts.append(begin)
        counts.append(count)

    def halo_copy(layer, j):
        return pltpu.make_async_remote_copy(
            src_ref=ybuf.at[layer, j], dst_ref=halo.at[layer, j],
            send_sem=hsend.at[layer, j], recv_sem=hrecv.at[layer, j],
            device_id=peer(1), device_id_type=MESH,
        )

    def part_copy(layer, k, j):
        return pltpu.make_async_remote_copy(
            src_ref=psend.at[layer, k, j], dst_ref=precv.at[layer, k, j],
            send_sem=qsend.at[layer, k, j], recv_sem=qrecv.at[layer, k, j],
            device_id=partner(k), device_id_type=MESH,
        )

    def stat_wait(layer, sem):
        every = stats.at[layer, pl.ds(1, T - 1)]
        pltpu.make_async_copy(every, every, sem.at[layer]).wait()

    lane_t = iota((128, ci), 0)
    member = lane_t % 32 == iota((128, ci), 1) // SIZE
    pick_sum = jnp.logical_and(member, lane_t < 64).astype(jnp.bfloat16)
    pick_sq = jnp.logical_and(member, lane_t >= 64).astype(jnp.bfloat16)
    lane_group = (iota((ci, 128), 1) % 32 == iota((ci, 128), 0) // SIZE).astype(jnp.bfloat16)

    def split(a):
        high = a.astype(jnp.bfloat16).astype(jnp.float32)
        rest = a - high
        middle = rest.astype(jnp.bfloat16).astype(jnp.float32)
        low = rest - middle
        return jnp.concatenate([high, middle, low, jnp.zeros_like(a)], axis=0).astype(jnp.bfloat16)

    def gather(parts, zero_one):
        r = dot(parts, zero_one)
        return (r[0:8] + r[8:16]) + r[16:24]

    def frame_sums(j, v):
        lines[j] = jnp.sum(v, axis=0, keepdims=True)
        lines[2 + j] = jnp.sum(v * v, axis=0, keepdims=True)

    def own_stats(layer):
        stacked = jnp.concatenate(
            [lines[q] for q in range(4)] + [jnp.zeros((4, ci), jnp.float32)], axis=0
        )
        by_group = gather(split(stacked), lane_group)
        own = iota((8, 128), 0) == iota((8, 128), 1) // 32
        stats[layer, 0] = jnp.sum(jnp.where(own, by_group, 0.0), axis=0, keepdims=True)

    def send_stats(layer):
        def go(d, carry):
            pltpu.make_async_remote_copy(
                src_ref=stats.at[layer, 0], dst_ref=stats.at[layer, d],
                send_sem=ssend.at[layer], recv_sem=srecv.at[layer],
                device_id=peer(d), device_id_type=MESH,
            ).start()
            return carry

        lax.fori_loop(1, T, go, 0, unroll=True)

    slot = iota((T, 1, 128), 0)
    frame = 2 * jnp.where(slot <= me, me - slot, me - slot + T) + (iota((T, 1, 128), 2) // 32) % 2

    def clip_stats(layer):
        stat_wait(layer, srecv)
        every = stats[layer]
        rows = []
        for f in range(4):
            inside = jnp.logical_and(frame >= starts[f], frame < starts[f] + counts[f])
            total = jnp.sum(jnp.where(inside, every, 0.0), axis=0)
            cells = jnp.maximum(counts[f], 1).astype(jnp.float32) * float(SIZE * CELLS)
            rows.append(total / jnp.full((1, 128), cells))
        parts = split(jnp.concatenate(rows + [jnp.zeros((4, 128), jnp.float32)], axis=0))
        mean = gather(parts, pick_sum)
        var = gather(parts, pick_sq) - mean * mean
        return mean, lax.rsqrt(var + EPS)

    column = iota((CELLS, ci), 0) % W

    def place(f, data, mean, scale, gamma, beta, slots):
        u = (data - mean[f : f + 1]) * (scale[f : f + 1] * gamma) + beta
        h = 0.5 * u * (1.0 + jnp.tanh(0.5 * u))
        before = jnp.where(column == 0, 0.0, pltpu.roll(h, 1, 0))
        after = jnp.where(column == W - 1, 0.0, pltpu.roll(h, CELLS - 1, 0))
        for kw, v in enumerate((before, h, after)):
            for kt, j in slots:
                if kt == 2:
                    kept = v
                else:
                    keep = jnp.full((CELLS, ci), starts[2 + j]) <= first + (j - 2 + kt)
                    kept = jnp.where(keep, v, 0.0)
                hs[kt, j, W : W + CELLS, kw * ci : (kw + 1) * ci] = kept.astype(jnp.bfloat16)

    def run_layer(layer, carry):
        mean, scale = clip_stats(layer)
        gamma, beta, bias = [par[3 * layer + q] for q in range(3)]
        for f, slots in ((2, [(2, 0), (1, 1)]), (3, [(2, 1)])):
            data = ybuf[layer, f - 2].astype(jnp.float32)
            place(f, data, mean, scale, gamma, beta, slots)
        for f, slots in ((0, [(0, 0)]), (1, [(1, 0), (0, 1)])):

            @pl.when(me > 0)
            def _():
                halo_copy(layer, f).wait_recv()

            data = halo[layer, f].astype(jnp.float32)
            place(f, data, mean, scale, gamma, beta, slots)

        def step(i, carry):
            k = lax.rem(i // 2 + 1, n)
            j = lax.rem(i, 2)

            @pl.when(j == 0)
            def _():
                w_copy(w1_ref, layer, k).wait()

            total = None
            for kt in range(3):
                pieces = [hs[kt, j, kh * W : kh * W + CELLS, :] for kh in range(3)]
                if ci % 128 == 0:
                    weights = wbuf[layer, k, 9 * kt : 9 * kt + 9].reshape(9 * ci, ci)
                    terms = [dot(jnp.concatenate(pieces, axis=1), weights)]
                else:
                    terms = [
                        dot(piece, wbuf[layer, k, 9 * kt + 3 * kh : 9 * kt + 3 * kh + 3].reshape(3 * ci, ci))
                        for kh, piece in enumerate(pieces)
                    ]
                for term in terms:
                    total = term if total is None else total + term

            @pl.when(k > 0)
            def _():
                psend[layer, k, j] = total.astype(jnp.bfloat16)
                part_copy(layer, k, j).start()

            @pl.when(k == 0)
            def _():
                out_ref[j] = total + bias

            return carry

        lax.fori_loop(0, 2 * n, step, 0)
        for j in range(2):
            z = out_ref[j]
            for k in range(1, n):
                part_copy(layer, k, j).wait_recv()
                z = z + precv[layer, k, j].astype(jnp.float32)
            y = z.astype(jnp.bfloat16)
            ybuf[layer + 1, j] = y
            out_ref[j] = z

            @pl.when(jnp.logical_and(layer == 0, me < T - 1))
            def _():
                halo_copy(1, j).start()

            frame_sums(j, y.astype(jnp.float32))

        @pl.when(layer == 0)
        def _():
            own_stats(1)
            send_stats(1)

        return carry

    for load in loads:
        load.wait()
    for j in range(2):
        frame_sums(j, ybuf[0, j].astype(jnp.float32))
    own_stats(0)
    pl.semaphore_wait(barrier, T - 1 + n - 1)
    send_stats(0)

    @pl.when(me < T - 1)
    def _():
        for j in range(2):
            halo_copy(0, j).start()

    lax.fori_loop(0, 2, run_layer, 0)
    out_ref[...] += ybuf[0].astype(jnp.float32)

    for layer in range(2):

        @pl.when(me < T - 1)
        def _():
            for j in range(2):
                halo_copy(layer, j).wait_send()

        stat_wait(layer, ssend)
        for k in range(1, n):
            for j in range(2):
                part_copy(layer, k, j).wait_send()


def on_device(n, T, x, lengths, g1, b1, w1, c1, g2, b2, w2, c2):
    ci, frames, cells = x.shape
    wide = ci % 128 == 0
    if wide:
        w1, w2 = [w.transpose(1, 0, 2) for w in (w1, w2)]
    else:
        w1, w2 = [w.reshape(ci, 27, n, ci).transpose(2, 1, 0, 3) for w in (w1, w2)]
    params = [v.reshape(1, ci) for v in (g1, b1, c1, g2, b2, c2)]
    hbm = pl.BlockSpec(memory_space=pl.ANY)
    dma = pltpu.SemaphoreType.DMA
    cube = (2, CELLS, ci)
    out = pl.pallas_call(
        functools.partial(kernel, n, T, lengths.shape[0], wide),
        out_shape=jax.ShapeDtypeStruct(cube, jnp.float32),
        in_specs=[pl.BlockSpec(memory_space=pltpu.SMEM)] + [hbm] * 9,
        out_specs=pl.BlockSpec(memory_space=pltpu.VMEM),
        scratch_shapes=[
            pltpu.VMEM((2, n, 27, ci, ci), jnp.bfloat16),
            pltpu.VMEM((3, 2, PAD, 3 * ci), jnp.bfloat16),
            pltpu.VMEM((2,) + cube, jnp.bfloat16),
            pltpu.VMEM((2, T, 1, 128), jnp.float32),
            pltpu.VMEM((4, 1, ci), jnp.float32),
            pltpu.VMEM((2, n) + cube, jnp.bfloat16),
            pltpu.VMEM((2, n) + cube, jnp.bfloat16),
            pltpu.VMEM((3,) + cube, jnp.bfloat16),
            pltpu.VMEM((6, 1, ci), jnp.float32),
            dma((2, n)),
            dma((7,)),
            dma((2, 2)),
            dma((2, 2)),
            dma((2,)),
            dma((2,)),
            dma((2, n, 2)),
            dma((2, n, 2)),
        ],
        compiler_params=pltpu.CompilerParams(
            collective_id=0, has_side_effects=True, vmem_limit_bytes=56 * 2**20
        ),
        cost_estimate=pl.CostEstimate(
            flops=4 * 27 * ci * C * 2 * CELLS, bytes_accessed=4 * 27 * ci * C, transcendentals=0
        ),
    )(lengths, x.transpose(1, 2, 0), *params, w1, w2)
    return out.transpose(2, 0, 1)


def solution(mesh):
    n, T = mesh.shape["chan"], mesh.shape["tm"]
    c = P("chan")
    cube = P("chan", None, None)
    data = P("chan", "tm", None)
    return jax.shard_map(
        functools.partial(on_device, n, T),
        mesh=mesh,
        in_specs=(data, P(), c, c, cube, c, c, c, cube, c),
        out_specs=data,
        check_vma=False,
    )
```

time: 48.6 us -> 38.8 us (0.80)
  Pallas kernels: 43.2 us -> 34.8 us
  local copies, waits for them, and re-layouts: 5.22 us -> 3.85 us
    pallas_call x1, Pallas kernels: 43.2 us -> 34.8 us  [on_device(): pl.pallas_call(functools.partial(kernel, n, T, lengths.shape[0], wide), o...]
    reshape x1 -> x0, local copies, waits for them, and re-layouts: 2.04 us -> none  [on_device(): return out.reshape(frames, cells, ci).transpose(2, 0, 1)]
    unnamed x0 -> x1, local copies, waits for them, and re-layouts: none -> 1.81 us
    another operation x2 -> x0, local copies, waits for them, and re-layouts: 1.37 us -> none  [on_device(): par = jnp.stack([g1, b1, c1, g2, b2, c2, zero, zero])]
where the time goes in v2:
time: 38.8 us; the launch traced here: 38.6 us
  Pallas kernels  34.8 us (90%)
  local copies, waits for them, and re-layouts  3.85 us (10%)
    pallas_call x1, Pallas kernels, on_device(): pl.pallas_call(functools.partial(kernel, n, T, lengths.shape[0], wide), o...  34.8 us
    transpose x1, local copies, waits for them, and re-layouts, on_device(): return out.transpose(2, 0, 1)  2.04 us
    unnamed x1, local copies, waits for them, and re-layouts  1.81 us

profile of v2, /device:TPU:0, one launch (start us, length us, event | category | flops | bytes accessed | tf_op | source)
XLA Modules:
  0.0 38.6 jit_solution(859484513008520111)
XLA Ops:
  0.0 1.8 %copy.11 = bf16[256,2,256]{0,2,1:T(8,128)(2,1)} copy(bf16[256,2,256]{2,1,0:T(2,128)(2,1)} %param.10) | data formatting | bytes 524288 | tf_op args[0]
  1.8 34.8 %shard_map.100 = f32[2,256,256]{2,1,0:T(8,128)} custom-call(s32[8]{0:T(128)} %len_ref.1, bf16[2,256,256]{2,1,0:T(8,128)(2,1)} %bitcast.11, f32[1,256]{1,0:T(1,128)} %bitcast.14, f32[1,256]{1,0:T(1,128)} %bitcast.15, f32[1,256]{1,0:T(1,128)} %bitcast.16, f32[1,256]{1,0:T(1,128)} %bitcast.17, f32[1,256]{1,0:T(1,128)} %bitcast.18, f32[1,256]{1,0:T(1,128)} %bitcast.19, ...), custom_call_target="tpu_custom_call" | custom-call | flops 7247757312 | bytes 14155776 | tf_op jit(solution)/shard_map/pallas_call | solution.py:299
  36.6 2.0 %copy.12 = f32[256,2,256]{2,1,0:T(2,128)} copy(f32[256,2,256]{0,2,1:T(8,128)} %bitcast.10) | data formatting | bytes 1048576 | tf_op jit(solution)/shard_map/transpose | solution.py:330

commit v3 on v2

--- a/solution.py
+++ b/solution.py
@@ -14,6 +14,7 @@
 W = 16
 CELLS = H * W
 PAD = CELLS + 2 * W
+HALF = CELLS // 2
 EPS = 1e-06
 MESH = pl.DeviceIdType.MESH
 
@@ -29,10 +30,10 @@
 def kernel(
     n, T, nclip, wide,
     len_ref, x_ref, g1_ref, b1_ref, c1_ref, g2_ref, b2_ref, c2_ref, w1_ref, w2_ref, out_ref,
-    wbuf, hs, halo, stats, lines, psend, precv, ybuf, par,
+    wbuf, hs, halo, stats, lines, psend, precv, ybuf, acc, x_half, x_full, par,
     w_sem, in_sem, hsend, hrecv, ssend, srecv, qsend, qrecv,
 ):
-    ci = x_ref.shape[2]
+    ci = x_ref.shape[0] // 4
     me = lax.axis_index("tm")
     ch = lax.axis_index("chan")
 
@@ -50,7 +51,7 @@
             src = w_ref.at[tgt]
         return pltpu.make_async_copy(src, wbuf.at[layer, k], w_sem.at[layer, k])
 
-    loads = [pltpu.make_async_copy(x_ref, ybuf.at[0], in_sem.at[6])] + [
+    loads = [pltpu.make_async_copy(x_ref, x_half, in_sem.at[6])] + [
         pltpu.make_async_copy(ref, par.at[i], in_sem.at[i])
         for i, ref in enumerate((g1_ref, b1_ref, c1_ref, g2_ref, b2_ref, c2_ref))
     ]
@@ -101,10 +102,14 @@
             device_id=peer(1), device_id_type=MESH,
         )
 
-    def part_copy(layer, k, j):
+    def part_copy(layer, k, piece):
+        if isinstance(piece, int) and piece == 2:
+            at = (layer, k, 1)
+        else:
+            at = (layer, k, 0, pl.ds(pl.multiple_of(piece * HALF, HALF), HALF))
         return pltpu.make_async_remote_copy(
-            src_ref=psend.at[layer, k, j], dst_ref=precv.at[layer, k, j],
-            send_sem=qsend.at[layer, k, j], recv_sem=qrecv.at[layer, k, j],
+            src_ref=psend.at[at], dst_ref=precv.at[at],
+            send_sem=qsend.at[layer, k, piece], recv_sem=qrecv.at[layer, k, piece],
             device_id=partner(k), device_id_type=MESH,
         )
 
@@ -200,17 +205,12 @@
             data = halo[layer, f].astype(jnp.float32)
             place(f, data, mean, scale, gamma, beta, slots)
 
-        def step(i, carry):
-            k = lax.rem(i // 2 + 1, n)
-            j = lax.rem(i, 2)
-
-            @pl.when(j == 0)
-            def _():
-                w_copy(w1_ref, layer, k).wait()
-
+        def block(k, j, row, count):
             total = None
             for kt in range(3):
-                pieces = [hs[kt, j, kh * W : kh * W + CELLS, :] for kh in range(3)]
+                pieces = [
+                    hs[kt, j, pl.ds(pl.multiple_of(row + kh * W, W), count), :] for kh in range(3)
+                ]
                 if ci % 128 == 0:
                     weights = wbuf[layer, k, 9 * kt : 9 * kt + 9].reshape(9 * ci, ci)
                     terms = [dot(jnp.concatenate(pieces, axis=1), weights)]
@@ -221,27 +221,62 @@
                     ]
                 for term in terms:
                     total = term if total is None else total + term
-
-            @pl.when(k > 0)
-            def _():
-                psend[layer, k, j] = total.astype(jnp.bfloat16)
-                part_copy(layer, k, j).start()
-
-            @pl.when(k == 0)
-            def _():
-                out_ref[j] = total + bias
-
+            return total
+
+        def early(i, carry):
+            k = i // 2 + 1
+            half = lax.rem(i, 2)
+
+            @pl.when(half == 0)
+            def _():
+                w_copy(w1_ref, layer, k).wait()
+
+            row = pl.multiple_of(half * HALF, HALF)
+            psend[layer, k, 0, pl.ds(row, HALF), :] = block(k, 0, row, HALF).astype(jnp.bfloat16)
+            part_copy(layer, k, half).start()
             return carry
 
-        lax.fori_loop(0, 2 * n, step, 0)
+        lax.fori_loop(0, 2 * (n - 1), early, 0)
+
+        def late(i, carry):
+            k = jnp.where(i < n, lax.rem(i + 1, n), 0)
+            j = jnp.where(i < n, 1, 0)
+
+            @pl.when(i == n - 1)
+            def _():
+                w_copy(w1_ref, layer, 0).wait()
+
+            total = block(k, j, 0, CELLS)
+
+            @pl.when(i < n - 1)
+            def _():
+                psend[layer, k, 1] = total.astype(jnp.bfloat16)
+                part_copy(layer, k, 2).start()
+
+            @pl.when(i >= n - 1)
+            def _():
+                acc[j] = total + bias
+
+            return carry
+
+        lax.fori_loop(0, n + 1, late, 0)
         for j in range(2):
-            z = out_ref[j]
+            z = acc[j]
             for k in range(1, n):
-                part_copy(layer, k, j).wait_recv()
+                for piece in ((0, 1), (2,))[j]:
+                    part_copy(layer, k, piece).wait_recv()
                 z = z + precv[layer, k, j].astype(jnp.float32)
             y = z.astype(jnp.bfloat16)
-            ybuf[layer + 1, j] = y
-            out_ref[j] = z
+
+            @pl.when(layer == 0)
+            def _():
+                ybuf[1, j] = y
+
+            @pl.when(layer == 1)
+            def _():
+                turned = (z + ybuf[0, j].astype(jnp.float32)).T
+                for q in range(2):
+                    out_ref[pl.ds(2 * q + j, ci, stride=4), :] = turned[:, q * 128 : q * 128 + 128]
 
             @pl.when(jnp.logical_and(layer == 0, me < T - 1))
             def _():
@@ -258,7 +293,11 @@
 
     for load in loads:
         load.wait()
+    x_full[...] = x_half[...].astype(jnp.float32)
     for j in range(2):
+        for q in range(2):
+            turned = x_full[pl.ds(2 * q + j, ci, stride=4), :].T
+            ybuf[0, j, q * 128 : q * 128 + 128, :] = turned.astype(jnp.bfloat16)
         frame_sums(j, ybuf[0, j].astype(jnp.float32))
     own_stats(0)
     pl.semaphore_wait(barrier, T - 1 + n - 1)
@@ -270,7 +309,6 @@
             halo_copy(0, j).start()
 
     lax.fori_loop(0, 2, run_layer, 0)
-    out_ref[...] += ybuf[0].astype(jnp.float32)
 
     for layer in range(2):
 
@@ -281,8 +319,13 @@
 
         stat_wait(layer, ssend)
         for k in range(1, n):
-            for j in range(2):
-                part_copy(layer, k, j).wait_send()
+            for piece in range(3):
+                part_copy(layer, k, piece).wait_send()
+
+
+def lines_of(x):
+    ci, frames, cells = x.shape
+    return x.reshape(ci, frames, 2, 128).transpose(0, 2, 1, 3).reshape(4 * ci, 128)
 
 
 def on_device(n, T, x, lengths, g1, b1, w1, c1, g2, b2, w2, c2):
@@ -298,7 +341,7 @@
     cube = (2, CELLS, ci)
     out = pl.pallas_call(
         functools.partial(kernel, n, T, lengths.shape[0], wide),
-        out_shape=jax.ShapeDtypeStruct(cube, jnp.float32),
+        out_shape=jax.ShapeDtypeStruct((4 * ci, 128), jnp.float32),
         in_specs=[pl.BlockSpec(memory_space=pltpu.SMEM)] + [hbm] * 9,
         out_specs=pl.BlockSpec(memory_space=pltpu.VMEM),
         scratch_shapes=[
@@ -309,7 +352,10 @@
             pltpu.VMEM((4, 1, ci), jnp.float32),
             pltpu.VMEM((2, n) + cube, jnp.bfloat16),
             pltpu.VMEM((2, n) + cube, jnp.bfloat16),
-            pltpu.VMEM((3,) + cube, jnp.bfloat16),
+            pltpu.VMEM((2,) + cube, jnp.bfloat16),
+            pltpu.VMEM(cube, jnp.float32),
+            pltpu.VMEM((4 * ci, 128), jnp.bfloat16),
+            pltpu.VMEM((4 * ci, 128), jnp.float32),
             pltpu.VMEM((6, 1, ci), jnp.float32),
             dma((2, n)),
             dma((7,)),
@@ -317,8 +363,8 @@
             dma((2, 2)),
             dma((2,)),
             dma((2,)),
-            dma((2, n, 2)),
-            dma((2, n, 2)),
+            dma((2, n, 3)),
+            dma((2, n, 3)),
         ],
         compiler_params=pltpu.CompilerParams(
             collective_id=0, has_side_effects=True, vmem_limit_bytes=56 * 2**20
@@ -326,8 +372,8 @@
         cost_estimate=pl.CostEstimate(
             flops=4 * 27 * ci * C * 2 * CELLS, bytes_accessed=4 * 27 * ci * C, transcendentals=0
         ),
-    )(lengths, x.transpose(1, 2, 0), *params, w1, w2)
-    return out.transpose(2, 0, 1)
+    )(lengths, lines_of(x), *params, w1, w2)
+    return out.reshape(ci, 2, frames, 128).transpose(0, 2, 1, 3).reshape(ci, frames, cells)
 
 
 def solution(mesh):

time: 38.8 us -> 36.3 us (0.936)
  local copies, waits for them, and re-layouts: 3.85 us -> 2.01 us
  Pallas kernels: 34.8 us -> 34.1 us
    transpose x1 -> x0, local copies, waits for them, and re-layouts: 2.04 us -> none  [on_device(): return out.transpose(2, 0, 1)]
    pallas_call x1, Pallas kernels: 34.8 us -> 34.1 us  [on_device(): pl.pallas_call(functools.partial(kernel, n, T, lengths.shape[0], wide), o...]
where the time goes in v3:
time: 36.3 us; the launch traced here: 36.1 us
  Pallas kernels  34.1 us (94%)
  local copies, waits for them, and re-layouts  2.01 us (6%)
    pallas_call x1, Pallas kernels, on_device(): pl.pallas_call(functools.partial(kernel, n, T, lengths.shape[0], wide), o...  34.1 us
    unnamed x1, local copies, waits for them, and re-layouts  2.01 us

profile of v3, /device:TPU:0, one launch (start us, length us, event | category | flops | bytes accessed | tf_op | source)
XLA Modules:
  0.0 36.1 jit_solution(15860602435248322507)
XLA Ops:
  0.0 34.1 %shard_map.100 = f32[1024,128]{1,0:T(8,128)} custom-call(s32[8]{0:T(128)} %len_ref.1, bf16[1024,128]{1,0:T(8,128)(2,1)} %bitcast.21, f32[1,256]{1,0:T(1,128)} %bitcast.22, f32[1,256]{1,0:T(1,128)} %bitcast.23, f32[1,256]{1,0:T(1,128)} %bitcast.24, f32[1,256]{1,0:T(1,128)} %bitcast.25, f32[1,256]{1,0:T(1,128)} %bitcast.26, f32[1,256]{1,0:T(1,128)} %bitcast.27, ...), custom_call_target="tpu_custom_call" | custom-call | flops 7247757312 | bytes 14155776 | tf_op jit(solution)/shard_map/pallas_call | solution.py:342
  34.1 2.0 %copy.14 = f32[256,2,256]{2,1,0:T(2,128)} copy(f32[256,2,256]{2,1,0:T(2,128)} %bitcast.18) | data formatting | bytes 1048576

commit v4 on v3

--- a/solution.py
+++ b/solution.py
@@ -14,7 +14,6 @@
 W = 16
 CELLS = H * W
 PAD = CELLS + 2 * W
-HALF = CELLS // 2
 EPS = 1e-06
 MESH = pl.DeviceIdType.MESH
 
@@ -51,22 +50,22 @@
             src = w_ref.at[tgt]
         return pltpu.make_async_copy(src, wbuf.at[layer, k], w_sem.at[layer, k])
 
+    barrier = pltpu.get_barrier_semaphore()
+
+    def greet(d, carry):
+        pl.semaphore_signal(barrier, inc=1, device_id=peer(d), device_id_type=MESH)
+        return carry
+
+    lax.fori_loop(1, T, greet, 0)
+    for k in range(1, n):
+        pl.semaphore_signal(barrier, inc=1, device_id=partner(k), device_id_type=MESH)
+
     loads = [pltpu.make_async_copy(x_ref, x_half, in_sem.at[6])] + [
         pltpu.make_async_copy(ref, par.at[i], in_sem.at[i])
         for i, ref in enumerate((g1_ref, b1_ref, c1_ref, g2_ref, b2_ref, c2_ref))
     ]
     for load in loads:
         load.start()
-
-    barrier = pltpu.get_barrier_semaphore()
-
-    def greet(d, carry):
-        pl.semaphore_signal(barrier, inc=1, device_id=peer(d), device_id_type=MESH)
-        return carry
-
-    lax.fori_loop(1, T, greet, 0)
-    for k in range(1, n):
-        pl.semaphore_signal(barrier, inc=1, device_id=partner(k), device_id_type=MESH)
 
     for layer, w_ref in enumerate((w1_ref, w2_ref)):
         for k in list(range(1, n)) + [0]:
@@ -102,14 +101,10 @@
             device_id=peer(1), device_id_type=MESH,
         )
 
-    def part_copy(layer, k, piece):
-        if isinstance(piece, int) and piece == 2:
-            at = (layer, k, 1)
-        else:
-            at = (layer, k, 0, pl.ds(pl.multiple_of(piece * HALF, HALF), HALF))
+    def part_copy(layer, k, j):
         return pltpu.make_async_remote_copy(
-            src_ref=psend.at[at], dst_ref=precv.at[at],
-            send_sem=qsend.at[layer, k, piece], recv_sem=qrecv.at[layer, k, piece],
+            src_ref=psend.at[layer, k, j], dst_ref=precv.at[layer, k, j],
+            send_sem=qsend.at[layer, k, j], recv_sem=qrecv.at[layer, k, j],
             device_id=partner(k), device_id_type=MESH,
         )
 
@@ -193,9 +188,8 @@
     def run_layer(layer, carry):
         mean, scale = clip_stats(layer)
         gamma, beta, bias = [par[3 * layer + q] for q in range(3)]
-        for f, slots in ((2, [(2, 0), (1, 1)]), (3, [(2, 1)])):
-            data = ybuf[layer, f - 2].astype(jnp.float32)
-            place(f, data, mean, scale, gamma, beta, slots)
+        data = ybuf[layer, 0].astype(jnp.float32)
+        place(2, data, mean, scale, gamma, beta, [(2, 0), (1, 1)])
         for f, slots in ((0, [(0, 0)]), (1, [(1, 0), (0, 1)])):
 
             @pl.when(me > 0)
@@ -205,11 +199,12 @@
             data = halo[layer, f].astype(jnp.float32)
             place(f, data, mean, scale, gamma, beta, slots)
 
-        def block(k, j, row, count):
+        def block(k, frames):
             total = None
             for kt in range(3):
                 pieces = [
-                    hs[kt, j, pl.ds(pl.multiple_of(row + kh * W, W), count), :] for kh in range(3)
+                    hs[kt, frames, kh * W : kh * W + CELLS, :].reshape(-1, 3 * ci)
+                    for kh in range(3)
                 ]
                 if ci % 128 == 0:
                     weights = wbuf[layer, k, 9 * kt : 9 * kt + 9].reshape(9 * ci, ci)
@@ -223,48 +218,30 @@
                     total = term if total is None else total + term
             return total
 
-        def early(i, carry):
+        def for_partner(i, carry):
             k = i // 2 + 1
-            half = lax.rem(i, 2)
-
-            @pl.when(half == 0)
+            j = lax.rem(i, 2)
+
+            @pl.when(j == 0)
             def _():
                 w_copy(w1_ref, layer, k).wait()
 
-            row = pl.multiple_of(half * HALF, HALF)
-            psend[layer, k, 0, pl.ds(row, HALF), :] = block(k, 0, row, HALF).astype(jnp.bfloat16)
-            part_copy(layer, k, half).start()
+            @pl.when(i == 1)
+            def _():
+                data = ybuf[layer, 1].astype(jnp.float32)
+                place(3, data, mean, scale, gamma, beta, [(2, 1)])
+
+            psend[layer, k, j] = block(k, j).astype(jnp.bfloat16)
+            part_copy(layer, k, j).start()
             return carry
 
-        lax.fori_loop(0, 2 * (n - 1), early, 0)
-
-        def late(i, carry):
-            k = jnp.where(i < n, lax.rem(i + 1, n), 0)
-            j = jnp.where(i < n, 1, 0)
-
-            @pl.when(i == n - 1)
-            def _():
-                w_copy(w1_ref, layer, 0).wait()
-
-            total = block(k, j, 0, CELLS)
-
-            @pl.when(i < n - 1)
-            def _():
-                psend[layer, k, 1] = total.astype(jnp.bfloat16)
-                part_copy(layer, k, 2).start()
-
-            @pl.when(i >= n - 1)
-            def _():
-                acc[j] = total + bias
-
-            return carry
-
-        lax.fori_loop(0, n + 1, late, 0)
+        lax.fori_loop(0, 2 * (n - 1), for_partner, 0)
+        w_copy(w1_ref, layer, 0).wait()
+        acc[...] = (block(0, slice(0, 2)) + bias).reshape(2, CELLS, ci)
         for j in range(2):
             z = acc[j]
             for k in range(1, n):
-                for piece in ((0, 1), (2,))[j]:
-                    part_copy(layer, k, piece).wait_recv()
+                part_copy(layer, k, j).wait_recv()
                 z = z + precv[layer, k, j].astype(jnp.float32)
             y = z.astype(jnp.bfloat16)
 
@@ -319,8 +296,8 @@
 
         stat_wait(layer, ssend)
         for k in range(1, n):
-            for piece in range(3):
-                part_copy(layer, k, piece).wait_send()
+            for j in range(2):
+                part_copy(layer, k, j).wait_send()
 
 
 def lines_of(x):
@@ -363,8 +340,8 @@
             dma((2, 2)),
             dma((2,)),
             dma((2,)),
-            dma((2, n, 3)),
-            dma((2, n, 3)),
+            dma((2, n, 2)),
+            dma((2, n, 2)),
         ],
         compiler_params=pltpu.CompilerParams(
             collective_id=0, has_side_effects=True, vmem_limit_bytes=56 * 2**20

time: 36.3 us -> 37.3 us (1.028)
  Pallas kernels: 34.1 us -> 35.1 us
    pallas_call x1, Pallas kernels: 34.1 us -> 35.1 us  [on_device(): pl.pallas_call(functools.partial(kernel, n, T, lengths.shape[0], wide), o...]
where the time goes in v4:
time: 37.3 us; the launch traced here: 37.2 us
  Pallas kernels  35.1 us (94%)
  local copies, waits for them, and re-layouts  2.01 us (5%)
    pallas_call x1, Pallas kernels, on_device(): pl.pallas_call(functools.partial(kernel, n, T, lengths.shape[0], wide), o...  35.1 us
    unnamed x1, local copies, waits for them, and re-layouts  2.01 us

profile of v4, /device:TPU:0, one launch (start us, length us, event | category | flops | bytes accessed | tf_op | source)
XLA Modules:
  0.0 37.2 jit_solution(4155842501135915767)
XLA Ops:
  0.0 35.1 %shard_map.100 = f32[1024,128]{1,0:T(8,128)} custom-call(s32[8]{0:T(128)} %len_ref.1, bf16[1024,128]{1,0:T(8,128)(2,1)} %bitcast.21, f32[1,256]{1,0:T(1,128)} %bitcast.22, f32[1,256]{1,0:T(1,128)} %bitcast.23, f32[1,256]{1,0:T(1,128)} %bitcast.24, f32[1,256]{1,0:T(1,128)} %bitcast.25, f32[1,256]{1,0:T(1,128)} %bitcast.26, f32[1,256]{1,0:T(1,128)} %bitcast.27, ...), custom_call_target="tpu_custom_call" | custom-call | flops 7247757312 | bytes 14155776 | tf_op jit(solution)/shard_map/pallas_call | solution.py:319
  35.2 2.0 %copy.14 = f32[256,2,256]{2,1,0:T(2,128)} copy(f32[256,2,256]{2,1,0:T(2,128)} %bitcast.18) | data formatting | bytes 1048576

commit v5 on v3

--- a/solution.py
+++ b/solution.py
@@ -51,22 +51,22 @@
             src = w_ref.at[tgt]
         return pltpu.make_async_copy(src, wbuf.at[layer, k], w_sem.at[layer, k])
 
+    barrier = pltpu.get_barrier_semaphore()
+
+    def greet(d, carry):
+        pl.semaphore_signal(barrier, inc=1, device_id=peer(d), device_id_type=MESH)
+        return carry
+
+    lax.fori_loop(1, T, greet, 0)
+    for k in range(1, n):
+        pl.semaphore_signal(barrier, inc=1, device_id=partner(k), device_id_type=MESH)
+
     loads = [pltpu.make_async_copy(x_ref, x_half, in_sem.at[6])] + [
         pltpu.make_async_copy(ref, par.at[i], in_sem.at[i])
         for i, ref in enumerate((g1_ref, b1_ref, c1_ref, g2_ref, b2_ref, c2_ref))
     ]
     for load in loads:
         load.start()
-
-    barrier = pltpu.get_barrier_semaphore()
-
-    def greet(d, carry):
-        pl.semaphore_signal(barrier, inc=1, device_id=peer(d), device_id_type=MESH)
-        return carry
-
-    lax.fori_loop(1, T, greet, 0)
-    for k in range(1, n):
-        pl.semaphore_signal(barrier, inc=1, device_id=partner(k), device_id_type=MESH)
 
     for layer, w_ref in enumerate((w1_ref, w2_ref)):
         for k in list(range(1, n)) + [0]:
@@ -193,9 +193,8 @@
     def run_layer(layer, carry):
         mean, scale = clip_stats(layer)
         gamma, beta, bias = [par[3 * layer + q] for q in range(3)]
-        for f, slots in ((2, [(2, 0), (1, 1)]), (3, [(2, 1)])):
-            data = ybuf[layer, f - 2].astype(jnp.float32)
-            place(f, data, mean, scale, gamma, beta, slots)
+        data = ybuf[layer, 0].astype(jnp.float32)
+        place(2, data, mean, scale, gamma, beta, [(2, 0), (1, 1)])
         for f, slots in ((0, [(0, 0)]), (1, [(1, 0), (0, 1)])):
 
             @pl.when(me > 0)
@@ -237,6 +236,8 @@
             return carry
 
         lax.fori_loop(0, 2 * (n - 1), early, 0)
+        data = ybuf[layer, 1].astype(jnp.float32)
+        place(3, data, mean, scale, gamma, beta, [(2, 1)])
 
         def late(i, carry):
             k = jnp.where(i < n, lax.rem(i + 1, n), 0)
@@ -321,6 +322,20 @@
         for k in range(1, n):
             for piece in range(3):
                 part_copy(layer, k, piece).wait_send()
+
+
+def hand_over(from_ref, to_ref, sems):
+    size = from_ref.shape[0] // 8
+    copies = [
+        pltpu.make_async_copy(
+            from_ref.at[pl.ds(i * size, size)], to_ref.at[pl.ds(i * size, size)], sems.at[i]
+        )
+        for i in range(8)
+    ]
+    for copy in copies:
+        copy.start()
+    for copy in copies:
+        copy.wait()
 
 
 def lines_of(x):
@@ -373,6 +388,14 @@
             flops=4 * 27 * ci * C * 2 * CELLS, bytes_accessed=4 * 27 * ci * C, transcendentals=0
         ),
     )(lengths, lines_of(x), *params, w1, w2)
+    out = pl.pallas_call(
+        hand_over,
+        out_shape=jax.ShapeDtypeStruct(out.shape, out.dtype),
+        in_specs=[hbm],
+        out_specs=hbm,
+        scratch_shapes=[dma((8,))],
+        compiler_params=pltpu.CompilerParams(vmem_limit_bytes=56 * 2**20),
+    )(out)
     return out.reshape(ci, 2, frames, 128).transpose(0, 2, 1, 3).reshape(ci, frames, cells)
 
 

time: 36.3 us -> 52.1 us (1.44)
  Pallas kernels: 34.1 us -> 51.9 us
  local copies, waits for them, and re-layouts: 2.01 us -> 0 us
    pallas_call x0 -> x1, Pallas kernels: none -> 17.1 us  [on_device(): pl.pallas_call(hand_over, out_shape=jax.ShapeDtypeStruct(out.shape, out.d...]
    unnamed x1 -> x0, local copies, waits for them, and re-layouts: 2.01 us -> none
    pallas_call x1, Pallas kernels: 34.1 us -> 34.9 us  [on_device(): pl.pallas_call(functools.partial(kernel, n, T, lengths.shape[0], wide), o...]
where the time goes in v5:
time: 52.1 us; the launch traced here: 51.9 us
  Pallas kernels  51.9 us (100%)
    pallas_call x1, Pallas kernels, on_device(): pl.pallas_call(functools.partial(kernel, n, T, lengths.shape[0], wide), o...  34.9 us
    pallas_call x1, Pallas kernels, on_device(): pl.pallas_call(hand_over, out_shape=jax.ShapeDtypeStruct(out.shape, out.d...  17.1 us

profile of v5, /device:TPU:0, one launch (start us, length us, event | category | flops | bytes accessed | tf_op | source)
XLA Modules:
  0.0 51.9 jit_solution(6960442414595624496)
XLA Ops:
  0.0 34.9 %shard_map.100.from_ref = f32[1024,128]{1,0:T(8,128)} custom-call(s32[8]{0:T(128)} %len_ref.1, bf16[1024,128]{1,0:T(8,128)(2,1)} %bitcast.20, f32[1,256]{1,0:T(1,128)} %bitcast.21, f32[1,256]{1,0:T(1,128)} %bitcast.22, f32[1,256]{1,0:T(1,128)} %bitcast.23, f32[1,256]{1,0:T(1,128)} %bitcast.24, f32[1,256]{1,0:T(1,128)} %bitcast.25, f32[1,256]{1,0:T(1,128)} %bitcast.26, ...), custom_call_target="tpu_custom_call" | custom-call | flops 7247757312 | bytes 14155776 | tf_op jit(solution)/shard_map/pallas_call | solution.py:357
  34.9 17.1 %shard_map.101 = f32[1024,128]{1,0:T(8,128)} custom-call(f32[1024,128]{1,0:T(8,128)} %shard_map.100.from_ref), custom_call_target="tpu_custom_call" | custom-call | tf_op jit(solution)/shard_map/pallas_call | solution.py:391

commit v6 on v3

--- a/solution.py
+++ b/solution.py
@@ -72,29 +72,6 @@
         for k in list(range(1, n)) + [0]:
             w_copy(w_ref, layer, k).start()
 
-    hs[:, :, 0:W, :] = jnp.zeros((3, 2, W, 3 * ci), jnp.bfloat16)
-    hs[:, :, W + CELLS :, :] = jnp.zeros((3, 2, W, 3 * ci), jnp.bfloat16)
-
-    @pl.when(me == 0)
-    def _():
-        halo[...] = jnp.zeros_like(halo)
-
-    first = 2 * me
-    starts, counts = [], []
-    for f in range(4):
-        g = first - 2 + f
-        begin = jnp.int32(0)
-        count = jnp.int32(0)
-        run = jnp.int32(0)
-        for c in range(nclip):
-            size = len_ref[c]
-            inside = jnp.logical_and(run <= g, g < run + size)
-            begin = jnp.where(inside, run, begin)
-            count = jnp.where(inside, size, count)
-            run = run + size
-        starts.append(begin)
-        counts.append(count)
-
     def halo_copy(layer, j):
         return pltpu.make_async_remote_copy(
             src_ref=ybuf.at[layer, j], dst_ref=halo.at[layer, j],
@@ -156,9 +133,6 @@
             return carry
 
         lax.fori_loop(1, T, go, 0, unroll=True)
-
-    slot = iota((T, 1, 128), 0)
-    frame = 2 * jnp.where(slot <= me, me - slot, me - slot + T) + (iota((T, 1, 128), 2) // 32) % 2
 
     def clip_stats(layer):
         stat_wait(layer, srecv)
@@ -291,8 +265,7 @@
 
         return carry
 
-    for load in loads:
-        load.wait()
+    loads[0].wait()
     x_full[...] = x_half[...].astype(jnp.float32)
     for j in range(2):
         for q in range(2):
@@ -308,6 +281,33 @@
         for j in range(2):
             halo_copy(0, j).start()
 
+    hs[:, :, 0:W, :] = jnp.zeros((3, 2, W, 3 * ci), jnp.bfloat16)
+    hs[:, :, W + CELLS :, :] = jnp.zeros((3, 2, W, 3 * ci), jnp.bfloat16)
+
+    @pl.when(me == 0)
+    def _():
+        halo[...] = jnp.zeros_like(halo)
+
+    first = 2 * me
+    starts, counts = [], []
+    for f in range(4):
+        g = first - 2 + f
+        begin = jnp.int32(0)
+        count = jnp.int32(0)
+        run = jnp.int32(0)
+        for c in range(nclip):
+            size = len_ref[c]
+            inside = jnp.logical_and(run <= g, g < run + size)
+            begin = jnp.where(inside, run, begin)
+            count = jnp.where(inside, size, count)
+            run = run + size
+        starts.append(begin)
+        counts.append(count)
+
+    slot = iota((T, 1, 128), 0)
+    frame = 2 * jnp.where(slot <= me, me - slot, me - slot + T) + (iota((T, 1, 128), 2) // 32) % 2
+    for load in loads[1:]:
+        load.wait()
     lax.fori_loop(0, 2, run_layer, 0)
 
     for layer in range(2):

time: 36.3 us -> 36.3 us (level)
  no operation moved by 1% of the time
where the time goes in v6:
time: 36.3 us; the launch traced here: 36.1 us
  Pallas kernels  34.1 us (94%)
  local copies, waits for them, and re-layouts  2.01 us (6%)
    pallas_call x1, Pallas kernels, on_device(): pl.pallas_call(functools.partial(kernel, n, T, lengths.shape[0], wide), o...  34.1 us
    unnamed x1, local copies, waits for them, and re-layouts  2.01 us

profile of v6, /device:TPU:0, one launch (start us, length us, event | category | flops | bytes accessed | tf_op | source)
XLA Modules:
  0.0 36.1 jit_solution(2522432153666965834)
XLA Ops:
  0.0 34.1 %shard_map.100 = f32[1024,128]{1,0:T(8,128)} custom-call(s32[8]{0:T(128)} %len_ref.1, bf16[1024,128]{1,0:T(8,128)(2,1)} %bitcast.21, f32[1,256]{1,0:T(1,128)} %bitcast.22, f32[1,256]{1,0:T(1,128)} %bitcast.23, f32[1,256]{1,0:T(1,128)} %bitcast.24, f32[1,256]{1,0:T(1,128)} %bitcast.25, f32[1,256]{1,0:T(1,128)} %bitcast.26, f32[1,256]{1,0:T(1,128)} %bitcast.27, ...), custom_call_target="tpu_custom_call" | custom-call | flops 7247757312 | bytes 14155776 | tf_op jit(solution)/shard_map/pallas_call | solution.py:342
  34.1 2.0 %copy.14 = f32[256,2,256]{2,1,0:T(2,128)} copy(f32[256,2,256]{2,1,0:T(2,128)} %bitcast.18) | data formatting | bytes 1048576
